TPU v7x, 32 devices: a whole 2x2x4 slice. The times are simulated.
32 devices in a mesh: grp: 2 (over x), row: 8 (over z, y), case: 2 (over core).
Axes of the slice: x: 2, y: 2, z: 4, core: 2. Of those that a mesh axis runs over, the one named last changes fastest.
Arguments:
- cotangent: float32 [768, 8192], P(('grp', 'case'), 'row'), parts along dimension 0, may hold values from -6 to 6
- rotor_index: int32 [768], P(('grp', 'case')), parts along dimension 0, may hold values from 0 to 127
- current_index: int32 [768], P(('grp', 'case')), parts along dimension 0, may hold values from 0 to 15
- position_table: float32 [256, 8192], P('grp', 'row'), parts along dimension 0, may hold values from -6 to 6
- current_table: float32 [32, 8192], P('grp', 'row'), parts along dimension 0, may hold values from -6 to 6
- segment_one: int32 [16384], P(('grp', 'row')), parts along dimension 0, may hold values from 0 to 63
- gain_one: float32 [128], P('grp'), parts along dimension 0, may hold values from 0.1 to 1.9
- field_one: float32 [768, 8192], P(('grp', 'case'), 'row'), parts along dimension 0, may hold values from -6 to 6
- scatter_one: float32 [16384, 8192], P(('grp', 'row'), 'case'), parts along dimension 0, may hold values from -0.0625 to 0.0625
- segment_zero: int32 [16384], P(('grp', 'case')), parts along dimension 0, may hold values from 0 to 63
- gain_zero: float32 [128], P('grp'), parts along dimension 0, may hold values from 0.1 to 1.9
- field_zero: float32 [768, 8192], P(('grp', 'row'), 'case'), parts along dimension 0, may hold values from -6 to 6
- scatter_zero: float32 [16384, 8192], P(('grp', 'case'), 'row'), parts along dimension 0, may hold values from -0.0625 to 0.0625
Outputs:
- adjoint_zero: float32 [768, 8192], P(('grp', 'case'), 'row'), parts along dimension 0
- grad_one: float32 [128], P('grp'), parts along dimension 0
- grad_zero: float32 [128], P('grp'), parts along dimension 0
There are 2 independent parts, one for each index of `grp`. A program takes and returns all parts, laid end to end along the dimension named above; each array names one. Nothing has to cross between parts.
All inputs are finite; a program needn't handle non-finite values.
Results may differ from a plain program's by a relative error of at most 0.00011.
Values sent between devices are 32-bit elements; how exact they have to be, the bound alone decides.
A program may use at most 128 MiB of HBM per device.

v0:
```python
import jax
import jax.numpy as jnp
from jax import lax
from jax.sharding import PartitionSpec as P


def lookup(which, lookup_table):
    onehot = (which[:, None] == jnp.arange(lookup_table.shape[0], dtype=jnp.int32)[None, :]).astype(
        jnp.float32
    )
    return jnp.dot(
        onehot, lookup_table, precision=lax.Precision.HIGHEST, preferred_element_type=jnp.float32
    )


def segment_rows(segment, gains):
    onehot = (segment[:, None] == jnp.arange(gains.shape[0], dtype=jnp.int32)[None, :]).astype(
        jnp.float32
    )
    return jnp.dot(
        onehot, gains, precision=lax.Precision.HIGHEST, preferred_element_type=jnp.float32
    )


def segment_total(values, segment, num_segments):
    onehot = (segment[:, None] == jnp.arange(num_segments, dtype=jnp.int32)[None, :]).astype(
        jnp.float32
    )
    return jnp.dot(
        values, onehot, precision=lax.Precision.HIGHEST, preferred_element_type=jnp.float32
    )


def local(
    cotangent,
    rotor_index,
    current_index,
    position_table,
    current_table,
    segment_one,
    gain_one,
    field_one,
    scatter_one,
    segment_zero,
    gain_zero,
    field_zero,
    scatter_zero,
):
    highest = lax.Precision.HIGHEST
    num_segments = gain_one.shape[0]
    adjoint_seed = (
        cotangent + lookup(rotor_index, position_table) + lookup(current_index, current_table)
    )
    scaled_two = adjoint_seed * segment_rows(segment_one, gain_one)[None, :]
    partial_one = segment_total(
        jnp.sum(adjoint_seed * field_one, axis=0), segment_one, num_segments
    )
    all_seeds = lax.all_gather(scaled_two, "case", axis=0, tiled=True)
    total_cases = all_seeds.shape[0]
    gains_zero = segment_rows(segment_zero, gain_zero)
    own_adjoint = lax.psum_scatter(
        jnp.dot(all_seeds, scatter_one, precision=highest, preferred_element_type=jnp.float32),
        "row",
        scatter_dimension=0,
        tiled=True,
    )
    scaled_one = own_adjoint * gains_zero[None, :]
    zero_terms = jnp.dot(
        lax.all_gather(scaled_one, "row", axis=0, tiled=True),
        scatter_zero,
        precision=highest,
        preferred_element_type=jnp.float32,
    )
    partial_zero = segment_total(
        jnp.sum(own_adjoint * field_zero, axis=0), segment_zero, num_segments
    )
    adjoint_zero = lax.psum_scatter(zero_terms, "case", scatter_dimension=0, tiled=True)
    grad_one, grad_zero = lax.psum((partial_one, partial_zero), ("row", "case"))
    return (adjoint_zero, grad_one / total_cases, grad_zero / total_cases)


def solution(mesh):
    placed = (
        P(("grp", "case"), "row"),
        P(("grp", "case")),
        P(("grp", "case")),
        P("grp", "row"),
        P("grp", "row"),
        P(("grp", "row")),
        P("grp"),
        P(("grp", "case"), "row"),
        P(("grp", "row"), "case"),
        P(("grp", "case")),
        P("grp"),
        P(("grp", "row"), "case"),
        P(("grp", "case"), "row"),
    )
    return jax.shard_map(
        local,
        mesh=mesh,
        in_specs=placed,
        out_specs=(P(("grp", "case"), "row"), P("grp"), P("grp")),
        check_vma=False,
    )
```

profile of v0, /device:TPU:0, one launch (start us, length us, event | category | flops | bytes accessed | tf_op | source)
XLA Modules:
  0.0 334.6 jit_solution(5923508530089032985)
XLA Ops:
  7.2 0.0 copy-start
  7.2 0.0 all-gather.3.cloned.1.call-start
  7.2 1.2 fusion.5
  8.4 0.0 copy-done
  8.4 1.7 convolution_add_fusion.1
  10.1 2.7 multiply_reduce_fusion.1
  12.8 0.0 all-gather.3.cloned.1.call-update
  12.8 0.0 reduce-scatter.3.cloned.1.call-start
  12.8 12.6 %all-gather.3.cloned.1.call-done = f32[384,1024]{1,0:T(8,128)} async-done(((f32[192,1024]{1,0:T(8,128)}), f32[384,1024]{1,0:T(8,128)}) %all-gather.3.cloned.1.call-update) | async-done | bytes 1572880 | tf_op jit(solution)/shard_map/all_gather | solution.py:58
  25.5 24.9 %fusion.12 = f32[384,4096]{1,0:T(8,128)} fusion(f32[384,1024]{1,0:T(8,128)} %all-gather.3.cloned.1.call-done, f32[1024,4096]{1,0:T(8,128)} %param.21), kind=kOutput, calls=%fused_computation.25 | convolution fusion | flops 19327352832 | bytes 24641536 | tf_op jit(solution)/shard_map/dot_general | solution.py:62
  50.4 0.0 copy-start.2
  50.4 0.0 copy-start.4
  50.4 0.0 copy-start.1
  50.4 0.0 reduce-scatter.3.cloned.1.call-update
  50.4 0.0 all-gather.5.cloned.1.call-start
  50.5 0.6 copy-done.2
  51.1 0.0 copy-done.4
  51.1 1.4 fusion.1
  52.5 117.1 %reduce-scatter.3.cloned.1.call-done = f32[48,4096]{1,0:T(8,128)} async-done(((f32[384,4096]{1,0:T(8,128)}), f32[48,4096]{1,0:T(8,128)}) %reduce-scatter.3.cloned.1.call-update) | async-done | bytes 786448 | tf_op jit(solution)/shard_map/reduce_scatter | solution.py:61
  169.7 0.0 copy-done.1
  169.7 2.1 multiply_reduce_fusion
  171.8 0.0 all-gather.5.cloned.1.call-update
  171.8 0.0 copy-start.3
  171.8 0.2 reduce-scatter.5.cloned.1.call-start
  172.0 98.6 %all-gather.5.cloned.1.call-done = f32[384,4096]{1,0:T(8,128)} async-done(((f32[48,4096]{1,0:T(8,128)}), f32[384,4096]{1,0:T(8,128)}) %all-gather.5.cloned.1.call-update) | async-done | bytes 6291472 | tf_op jit(solution)/shard_map/all_gather | solution.py:69
  270.6 24.9 %fusion.13 = f32[384,1024]{1,0:T(8,128)} fusion(f32[384,4096]{1,0:T(8,128)} %all-gather.5.cloned.1.call-done, f32[4096,1024]{1,0:T(8,128)} %param.25), kind=kOutput, calls=%fused_computation.26 | convolution fusion | flops 19327352832 | bytes 24641536 | tf_op jit(solution)/shard_map/dot_general | solution.py:68
  295.5 0.0 reduce-scatter.5.cloned.1.call-update
  295.6 0.0 copy-done.3
  295.6 0.4 convolution_bitcast_fusion
  295.9 1.0 fusion.2
  296.9 30.6 %all-reduce = (f32[64]{0:T(128)S(1)}, f32[64]{0:T(128)S(1)}) all-reduce(f32[64]{0:T(128)S(1)} %convolution_bitcast_fusion, f32[64]{0:T(128)S(1)} %fusion.2), channel_id=1, replica_groups=mesh['grp'=2,'row'=8,'case'=2] {'row','case'}, use_global_device_ids=true, to_apply=%region_3.0 | all-reduce | flops 128 | bytes 1024 | tf_op jit(solution)/shard_map/psum | solution.py:78
  327.5 0.5 broadcast_multiply_fusion.2
  328.0 0.0 reduce-scatter.5.cloned.1.call-done
Async XLA Ops:
  7.2 1.2 copy-start
  7.2 18.3 %all-gather.3.cloned.1.call-start = ((), (), s32[]{:S(2)}) async-start(), calls=%async_computation.2 | async-start | bytes 2359296 | tf_op jit(solution)/shard_map/all_gather | solution.py:58
  12.8 156.9 %reduce-scatter.3.cloned.1.call-start = ((), (), s32[]{:S(2)}) async-start(), calls=%async_computation.3 | async-start | bytes 7077888 | tf_op jit(solution)/shard_map/reduce_scatter | solution.py:61
  50.4 0.7 copy-start.2
  50.4 0.7 copy-start.4
  50.4 119.3 %copy-start.1 = (f32[48,4096]{1,0:T(8,128)S(1)}, f32[48,4096]{1,0:T(8,128)}, u32[]{:S(2)}) copy-start(f32[48,4096]{1,0:T(8,128)} %param.24) | copy-start | bytes 2359300
  50.4 220.2 %all-gather.5.cloned.1.call-start = ((), (), s32[]{:S(2)}) async-start(), calls=%async_computation.4 | async-start | bytes 7077888 | tf_op jit(solution)/shard_map/all_gather | solution.py:69
  171.8 123.8 %copy-start.3 = (s32[1024]{0:T(1024)S(1)}, s32[1024]{0:T(1024)}, u32[]{:S(2)}) copy-start(s32[1024]{0:T(1024)} %param.18) | copy-start | bytes 12292
  171.8 156.2 %reduce-scatter.5.cloned.1.call-start = ((), (), s32[]{:S(2)}) async-start(), calls=%async_computation.5 | async-start | bytes 2359296 | tf_op jit(solution)/shard_map/reduce_scatter | solution.py:77
Sparse Core Ops, SparseCore 0:
  12.9 12.4 all-gather.2
  50.5 119.0 reduce-scatter.2
  172.4 98.1 all-gather.4
  295.7 7.2 reduce-scatter.4
where the time goes:
time: 335 us
  waiting for transfers between devices  228 us (68%)
  matrix products  58.1 us (17%)
  blocking collectives  30.6 us (9%)
  between operations  13.8 us (4%)
    reduce_scatter x1, waiting for transfers between devices, local(): lax.psum_scatter(jnp.dot(all_seeds, scatter_one, precision=highest, prefe...  117 us
    all_gather x1, waiting for transfers between devices, local(): lax.all_gather(scaled_one, 'row', axis=0, tiled=True)  98.6 us
    psum x1, blocking collectives, local(): grad_one, grad_zero = lax.psum((partial_one, partial_zero), ('row', 'case'))  30.6 us
    dot_general x1, matrix products, local(): jnp.dot(all_seeds, scatter_one, precision=highest, preferred_element_type...  24.9 us
    dot_general x1, matrix products, local(): jnp.dot(lax.all_gather(scaled_one, 'row', axis=0, tiled=True), scatter_ze...  24.9 us
    all_gather x1, waiting for transfers between devices, local(): all_seeds = lax.all_gather(scaled_two, 'case', axis=0, tiled=True)  12.6 us
  transfers between devices with their start and end apart: 4, of which 3 were waited for; matrix products, arithmetic and copies ran while one was open for 1% of the time, Pallas kernels for 0%

commit v1 on v0

v1 whole, which is shorter than its diff:
```python
import functools

import jax
import jax.numpy as jnp
from jax import lax
from jax.experimental import pallas as pl
from jax.experimental.pallas import tpu as pltpu
from jax.sharding import PartitionSpec as P

MESH = pl.DeviceIdType.MESH
LANES = 128
SUBS = 2


def lookup(which, lookup_table):
    onehot = (which[:, None] == jnp.arange(lookup_table.shape[0], dtype=jnp.int32)[None, :]).astype(
        jnp.float32
    )
    return jnp.dot(
        onehot, lookup_table, precision=lax.Precision.HIGHEST, preferred_element_type=jnp.float32
    )


def segment_rows(segment, gains):
    onehot = (segment[:, None] == jnp.arange(gains.shape[0], dtype=jnp.int32)[None, :]).astype(
        jnp.float32
    )
    return jnp.dot(
        onehot, gains, precision=lax.Precision.HIGHEST, preferred_element_type=jnp.float32
    )


def segment_total(values, segment, num_segments):
    onehot = (segment[:, None] == jnp.arange(num_segments, dtype=jnp.int32)[None, :]).astype(
        jnp.float32
    )
    return jnp.dot(
        values, onehot, precision=lax.Precision.HIGHEST, preferred_element_type=jnp.float32
    )


def split(x):
    high = x.astype(jnp.bfloat16)
    return high, (x - high.astype(jnp.float32)).astype(jnp.bfloat16)


def dot3(a_high, a_low, b_high, b_low):
    dot = functools.partial(jnp.dot, preferred_element_type=jnp.float32)
    return dot(a_low, b_high) + dot(a_high, b_low) + dot(a_high, b_high)


def ring_kernel(
    n, cot, rot, cur, ptab, ctab, seg1, gain1, f1, s1, seg0, gain0, f0, s0,
    out, g1_out, g0_out,
    own, peer, a_high, a_low, s1_buf, s0_buf, ring, part, total, other, g0,
    send_sem, recv_sem, s1_sem, s0_sem, pair_send, pair_recv,
):
    row, case = lax.axis_index("row"), lax.axis_index("case")
    half = n // 2
    upper = lax.rem(row, 2)
    place = (row // 2) * (1 - upper) + (n - 1 - row // 2) * upper

    def row_at(position):
        position = lax.rem(position + n, n)
        far = position // half
        return (1 - far) * 2 * position + far * (2 * (n - 1 - position) + 1)

    right, left = row_at(place + 1), row_at(place - 1)
    targets = (right, left)
    local_cases = cot.shape[0]
    cases = 2 * local_cases
    width = ring.shape[3]
    sub = cases // SUBS
    field_cases = f0.shape[0]
    segments = gain1.shape[0]

    def chunk(step, d):
        c = lax.rem(place + 2 * n - step, n) if d == 0 else lax.rem(place + step, n)
        return 2 * c + d

    def second_chunk(t, d):
        return chunk(t + n - 1, d)

    def s1_copy(step, d):
        start = pl.multiple_of(chunk(step, d) * width, width)
        return pltpu.make_async_copy(
            s1.at[:, pl.ds(start, width)], s1_buf.at[2 * step + d], s1_sem.at[2 * step + d]
        )

    def s0_copy(t, d):
        start = pl.multiple_of(second_chunk(t, d) * width, width)
        return pltpu.make_async_copy(
            s0.at[pl.ds(start, width)], s0_buf.at[2 * t + d], s0_sem.at[2 * t + d]
        )

    def ring_copy(step, d, h):
        rows = pl.ds(h * sub, sub)
        return pltpu.make_async_remote_copy(
            src_ref=ring.at[step, d, rows],
            dst_ref=ring.at[step + 1, d, rows],
            send_sem=send_sem.at[step, d, h],
            recv_sem=recv_sem.at[step + 1, d, h],
            device_id={"row": targets[d]},
            device_id_type=MESH,
        )

    def pair_copy(src, dst, at):
        return pltpu.make_async_remote_copy(
            src_ref=src,
            dst_ref=dst,
            send_sem=pair_send.at[at],
            recv_sem=pair_recv.at[at],
            device_id={"case": 1 - case},
            device_id_type=MESH,
        )

    barrier = pltpu.get_barrier_semaphore()
    pl.semaphore_signal(barrier, inc=1, device_id={"row": left}, device_id_type=MESH)
    pl.semaphore_signal(barrier, inc=1, device_id={"row": right}, device_id_type=MESH)
    pl.semaphore_signal(barrier, inc=1, device_id={"case": 1 - case}, device_id_type=MESH)

    for step in range(n):
        for d in range(2):
            s1_copy(step, d).start()

    highest = functools.partial(
        jnp.dot, precision=lax.Precision.HIGHEST, preferred_element_type=jnp.float32
    )

    def pick(index, count):
        ids = lax.broadcasted_iota(jnp.int32, (local_cases, count), 1)
        return jnp.where(ids == index, 1.0, 0.0).astype(jnp.float32)

    def members(segment):
        return lax.broadcasted_iota(jnp.int32, (segments, segment.shape[1]), 0) == segment

    def gain_row(segment, gains):
        return jnp.sum(jnp.where(members(segment), gains, 0.0), axis=0, keepdims=True)

    def fold(values):
        folded = values[:, :LANES]
        for at in range(LANES, values.shape[1], LANES):
            folded = folded + values[:, at : at + LANES]
        return folded

    seed = (
        cot[...]
        + highest(pick(rot[...], ptab.shape[0]), ptab[...])
        + highest(pick(cur[...], ctab.shape[0]), ctab[...])
    )
    own[...] = seed * gain_row(seg1[...], gain1[...])
    pl.semaphore_wait(barrier, 3)
    pair_copy(own, peer, 0).start()
    mine = pl.ds(pl.multiple_of(case * local_cases, local_cases), local_cases)
    theirs = pl.ds(pl.multiple_of((1 - case) * local_cases, local_cases), local_cases)
    a_high[mine], a_low[mine] = split(own[...])
    column = jnp.sum(seed * f1[...], axis=0, keepdims=True)
    picked = fold(jnp.where(members(seg1[...]), column, 0.0))
    g1_out[...] = jnp.sum(picked, axis=1, keepdims=True)
    g0[...] = jnp.zeros_like(g0)
    total[...] = jnp.zeros_like(total)
    pair_copy(own, peer, 0).wait_recv()
    a_high[theirs], a_low[theirs] = split(peer[...])

    def product(step, d):
        s1_copy(step, d).wait()
        b_high, b_low = split(s1_buf[2 * step + d])
        return dot3(a_high[...], a_low[...], b_high, b_low)

    for d in range(2):
        ring[0, d] = product(0, d)
        for h in range(SUBS):
            ring_copy(0, d, h).start()
    for t in range(n):
        for d in range(2):
            s0_copy(t, d).start()

    def reduce_step(step, carry):
        for d in range(2):
            part[d] = product(step, d)
        for h in range(SUBS):
            for d in range(2):
                rows = pl.ds(h * sub, sub)
                ring_copy(step - 1, d, h).wait_recv()
                ring[step, d, rows] = ring[step, d, rows] + part[d, rows]
                ring_copy(step, d, h).start()
        return carry

    lax.fori_loop(1, n, reduce_step, 0)

    def second(t, rows):
        for d in range(2):
            start = pl.multiple_of(second_chunk(t, d) * width, width)
            segment = seg0[:, pl.ds(start, width)]
            x_high, x_low = split(ring[n - 1 + t, d, rows] * gain_row(segment, gain0[...]))
            b_high, b_low = split(s0_buf[2 * t + d])
            total[rows] = total[rows] + dot3(x_high, x_low, b_high, b_low)

    def gradient(t):
        for d in range(2):
            start = pl.multiple_of(second_chunk(t, d) * width, width)
            segment = seg0[:, pl.ds(start, width)]
            at = pl.multiple_of(row * field_cases, 8)
            column = jnp.sum(
                ring[n - 1 + t, d, pl.ds(at, field_cases)] * f0[:, pl.ds(start, width)],
                axis=0,
                keepdims=True,
            )
            g0[...] = g0[...] + fold(jnp.where(members(segment), column, 0.0))

    def gather_step(t, carry):
        for d in range(2):
            s0_copy(t, d).wait()
        second(t, pl.ds(0, cases))
        gradient(t)
        step = n + t
        for h in range(SUBS):
            for d in range(2):
                ring_copy(step - 1, d, h).wait_recv()

                @pl.when(t < n - 2)
                def _():
                    ring_copy(step, d, h).start()

        return carry

    lax.fori_loop(0, n - 1, gather_step, 0)
    for d in range(2):
        s0_copy(n - 1, d).wait()
    second(n - 1, theirs)
    pair_copy(total.at[theirs], other, 1).start()
    second(n - 1, mine)
    gradient(n - 1)
    g0_out[...] = jnp.sum(g0[...], axis=1, keepdims=True)
    pair_copy(total.at[theirs], other, 1).wait_recv()
    out[...] = total[mine] + other[...]

    pair_copy(own, peer, 0).wait_send()
    pair_copy(total.at[theirs], other, 1).wait_send()

    def drain(step, carry):
        for d in range(2):
            for h in range(SUBS):
                ring_copy(step, d, h).wait_send()
        return carry

    lax.fori_loop(0, 2 * n - 2, drain, 0)


def ring_call(n, args):
    (cot, rot, cur, ptab, ctab, seg1, gain1, f1, s1, seg0, gain0, f0, s0) = args
    local_cases, depth = cot.shape
    cases = 2 * local_cases
    columns = s1.shape[1]
    width = columns // (2 * n)
    segments = gain1.shape[0]
    vmem = pl.BlockSpec(memory_space=pltpu.VMEM)
    hbm = pl.BlockSpec(memory_space=pl.ANY)
    f32, bf16 = jnp.float32, jnp.bfloat16
    dma = pltpu.SemaphoreType.DMA
    return pl.pallas_call(
        functools.partial(ring_kernel, n),
        out_shape=(
            jax.ShapeDtypeStruct((local_cases, depth), f32),
            jax.ShapeDtypeStruct((segments, 1), f32),
            jax.ShapeDtypeStruct((segments, 1), f32),
        ),
        in_specs=[vmem] * 8 + [hbm] + [vmem] * 3 + [hbm],
        out_specs=(vmem, vmem, vmem),
        scratch_shapes=[
            pltpu.VMEM((local_cases, depth), f32),
            pltpu.VMEM((local_cases, depth), f32),
            pltpu.VMEM((cases, depth), bf16),
            pltpu.VMEM((cases, depth), bf16),
            pltpu.VMEM((2 * n, depth, width), f32),
            pltpu.VMEM((2 * n, width, depth), f32),
            pltpu.VMEM((2 * n - 1, 2, cases, width), f32),
            pltpu.VMEM((2, cases, width), f32),
            pltpu.VMEM((cases, depth), f32),
            pltpu.VMEM((local_cases, depth), f32),
            pltpu.VMEM((segments, LANES), f32),
            dma((2 * n - 1, 2, SUBS)),
            dma((2 * n - 1, 2, SUBS)),
            dma((2 * n,)),
            dma((2 * n,)),
            dma((2,)),
            dma((2,)),
        ],
        compiler_params=pltpu.CompilerParams(
            collective_id=0, has_side_effects=True, vmem_limit_bytes=62 * 1024 * 1024
        ),
        cost_estimate=pl.CostEstimate(
            flops=12 * cases * depth * columns, bytes_accessed=12 * depth * columns, transcendentals=0
        ),
    )(
        cot, rot[:, None], cur[:, None], ptab, ctab, seg1[None, :], gain1[:, None], f1, s1,
        seg0[None, :], gain0[:, None], f0, s0,
    )


def local(n, *args):
    (cot, rot, cur, ptab, ctab, seg1, gain1, f1, s1, seg0, gain0, f0, s0) = args
    width = s1.shape[1] // (2 * n)
    if n % 2 == 0 and width % LANES == 0 and width * 2 * n == s1.shape[1]:
        adjoint_zero, partial_one, partial_zero = ring_call(n, args)
        partial_one, partial_zero = partial_one[:, 0], partial_zero[:, 0]
        total_cases = 2 * cot.shape[0]
    else:
        highest = lax.Precision.HIGHEST
        num_segments = gain1.shape[0]
        adjoint_seed = cot + lookup(rot, ptab) + lookup(cur, ctab)
        scaled_two = adjoint_seed * segment_rows(seg1, gain1)[None, :]
        partial_one = segment_total(jnp.sum(adjoint_seed * f1, axis=0), seg1, num_segments)
        all_seeds = lax.all_gather(scaled_two, "case", axis=0, tiled=True)
        total_cases = all_seeds.shape[0]
        own_adjoint = lax.psum_scatter(
            jnp.dot(all_seeds, s1, precision=highest, preferred_element_type=jnp.float32),
            "row",
            scatter_dimension=0,
            tiled=True,
        )
        scaled_one = own_adjoint * segment_rows(seg0, gain0)[None, :]
        zero_terms = jnp.dot(
            lax.all_gather(scaled_one, "row", axis=0, tiled=True),
            s0,
            precision=highest,
            preferred_element_type=jnp.float32,
        )
        partial_zero = segment_total(jnp.sum(own_adjoint * f0, axis=0), seg0, num_segments)
        adjoint_zero = lax.psum_scatter(zero_terms, "case", scatter_dimension=0, tiled=True)
    grad_one, grad_zero = lax.psum((partial_one, partial_zero), ("row", "case"))
    return (adjoint_zero, grad_one / total_cases, grad_zero / total_cases)


def solution(mesh):
    placed = (
        P(("grp", "case"), "row"),
        P(("grp", "case")),
        P(("grp", "case")),
        P("grp", "row"),
        P("grp", "row"),
        P(("grp", "row")),
        P("grp"),
        P(("grp", "case"), "row"),
        P(("grp", "row"), "case"),
        P(("grp", "case")),
        P("grp"),
        P(("grp", "row"), "case"),
        P(("grp", "case"), "row"),
    )
    return jax.shard_map(
        functools.partial(local, mesh.shape["row"]),
        mesh=mesh,
        in_specs=placed,
        out_specs=(P(("grp", "case"), "row"), P("grp"), P("grp")),
        check_vma=False,
    )
```

time: 335 us -> 179 us (0.53)
  waiting for transfers between devices: 228 us -> 0 us
  Pallas kernels: 0 us -> 135 us
  matrix products: 58.1 us -> 0 us
  between operations: 13.8 us -> 0.64 us
  local copies, waits for them, and re-layouts: 0.66 us -> 7.65 us
    pallas_call x0 -> x1, Pallas kernels: none -> 135 us  [ring_call(): pl.pallas_call(functools.partial(ring_kernel, n), out_shape=(jax.ShapeDty...]
    reduce_scatter x2 -> x0, waiting for transfers between devices: 117 us -> none  [the longest x1 117 us: local(): lax.psum_scatter(jnp.dot(all_seeds, scatter_one, precision=highest, prefe...]
    all_gather x2 -> x0, waiting for transfers between devices: 111 us -> none  [the longest x1 98.6 us: local(): lax.all_gather(scaled_one, 'row', axis=0, tiled=True)]
    dot_general x8 -> x0, matrix products: 58.1 us -> none  [the longest x1 24.9 us: local(): jnp.dot(all_seeds, scatter_one, precision=highest, preferred_element_type...]
    broadcast_in_dim x0 -> x4, local copies, waits for them, and re-layouts: none -> 5.57 us  [the longest x1 1.44 us: ring_call(): rot[:, None]]
  transfers between devices with their start and end apart: 4 -> 0, of which waited for: 3 -> 0; matrix products, arithmetic and copies ran while one was open for 1% -> 0% of each run, Pallas kernels for 0% -> 0%
where the time goes in v1:
time: 179 us
  Pallas kernels  135 us (75%)
  blocking collectives  32.9 us (18%)
  local copies, waits for them, and re-layouts  7.65 us (4%)
  other arithmetic  2.26 us (1%)
    pallas_call x1, Pallas kernels, ring_call(): pl.pallas_call(functools.partial(ring_kernel, n), out_shape=(jax.ShapeDty...  135 us
    psum x1, blocking collectives, local(): grad_one, grad_zero = lax.psum((partial_one, partial_zero), ('row', 'case'))  32.9 us

profile of v1, /device:TPU:0, one launch (start us, length us, event | category | flops | bytes accessed | tf_op | source)
XLA Modules:
  0.0 179.0 jit_solution(3512674476135684582)
XLA Ops:
  0.6 1.4 copy.18.rot
  2.1 1.4 copy.19.cur
  3.5 1.3 copy.20.gain1
  4.9 1.3 copy.21.gain0
  6.2 135.5 %shard_map.148 = (f32[192,1024]{1,0:T(8,128)}, f32[64,1]{1,0:T(8,128)}, f32[64,1]{1,0:T(8,128)}) custom-call(f32[192,1024]{1,0:T(8,128)} %cot.1, s32[192,1]{1,0:T(8,128)} %copy.18.rot, s32[192,1]{1,0:T(8,128)} %copy.19.cur, f32[128,1024]{1,0:T(8,128)} %ptab.1, f32[16,1024]{1,0:T(8,128)} %ctab.1, s32[1,1024]{1,0:T(1,128)} %bitcast.11, f32[64,1]{1,0:T(8,128)} %copy.20.gain1, ...), custom_call_target="tpu_custom_call" | custom-call | flops 19327352832 | bytes 50331648 | tf_op jit(solution)/shard_map/pallas_call | solution.py:261
  141.7 0.9 reduce
  142.6 0.9 reduce.1
  143.4 32.9 %all-reduce = (f32[64]{0:T(128)S(1)}, f32[64]{0:T(128)S(1)}) all-reduce(f32[64]{0:T(128)S(1)} %reduce, f32[64]{0:T(128)S(1)} %reduce.1), channel_id=1, replica_groups=mesh['grp'=2,'row'=8,'case'=2] {'row','case'}, use_global_device_ids=true, to_apply=%region_0.0 | all-reduce | flops 128 | bytes 1024 | tf_op jit(solution)/shard_map/psum | solution.py:331
  176.3 0.5 broadcast_multiply_fusion
  176.9 2.1 %copy.23 = f32[192,1024]{1,0:T(8,128)} copy(f32[192,1024]{1,0:T(8,128)} %get-tuple-element.16) | data formatting | bytes 1572864

commit v2 on v1

--- a/solution.py
+++ b/solution.py
@@ -9,7 +9,7 @@
 
 MESH = pl.DeviceIdType.MESH
 LANES = 128
-SUBS = 2
+SUBS = 4
 
 
 def lookup(which, lookup_table):
@@ -52,8 +52,8 @@
 def ring_kernel(
     n, cot, rot, cur, ptab, ctab, seg1, gain1, f1, s1, seg0, gain0, f0, s0,
     out, g1_out, g0_out,
-    own, peer, a_high, a_low, s1_buf, s0_buf, ring, part, total, other, g0,
-    send_sem, recv_sem, s1_sem, s0_sem, pair_send, pair_recv,
+    own, peer, a_high, a_low, s1_buf, s0_buf, ring, part, total, other, g1, g0, pair_grads, row_grads,
+    send_sem, recv_sem, s1_sem, s0_sem, pair_send, pair_recv, row_send, row_recv,
 ):
     row, case = lax.axis_index("row"), lax.axis_index("case")
     half = n // 2
@@ -72,7 +72,7 @@
     width = ring.shape[3]
     sub = cases // SUBS
     field_cases = f0.shape[0]
-    segments = gain1.shape[0]
+    segments = gain1.shape[1]
 
     def chunk(step, d):
         c = lax.rem(place + 2 * n - step, n) if d == 0 else lax.rem(place + step, n)
@@ -114,9 +114,32 @@
             device_id_type=MESH,
         )
 
+    def row_copy(k):
+        return pltpu.make_async_remote_copy(
+            src_ref=row_grads.at[row],
+            dst_ref=row_grads.at[row],
+            send_sem=row_send.at[k],
+            recv_sem=row_recv.at[row],
+            device_id={"row": lax.rem(row + k, n)},
+            device_id_type=MESH,
+        )
+
+    def row_arrival(k):
+        source = lax.rem(row + k, n)
+        return pltpu.make_async_remote_copy(
+            src_ref=row_grads.at[source],
+            dst_ref=row_grads.at[source],
+            send_sem=row_send.at[k],
+            recv_sem=row_recv.at[source],
+            device_id={"row": source},
+            device_id_type=MESH,
+        )
+
     barrier = pltpu.get_barrier_semaphore()
-    pl.semaphore_signal(barrier, inc=1, device_id={"row": left}, device_id_type=MESH)
-    pl.semaphore_signal(barrier, inc=1, device_id={"row": right}, device_id_type=MESH)
+    for k in range(1, n):
+        pl.semaphore_signal(
+            barrier, inc=1, device_id={"row": lax.rem(row + k, n)}, device_id_type=MESH
+        )
     pl.semaphore_signal(barrier, inc=1, device_id={"case": 1 - case}, device_id_type=MESH)
 
     for step in range(n):
@@ -129,7 +152,20 @@
 
     def pick(index, count):
         ids = lax.broadcasted_iota(jnp.int32, (local_cases, count), 1)
-        return jnp.where(ids == index, 1.0, 0.0).astype(jnp.float32)
+        column = upright(index.astype(jnp.float32)).astype(jnp.int32)
+        return jnp.where(ids == column, 1.0, 0.0).astype(jnp.float32)
+
+    def diagonal(size):
+        down = lax.broadcasted_iota(jnp.int32, (size, size), 0)
+        return down == lax.broadcasted_iota(jnp.int32, (size, size), 1)
+
+    def upright(values):
+        return jnp.sum(jnp.where(diagonal(values.shape[1]), values, 0.0), axis=1, keepdims=True)
+
+    def flat(values):
+        return jnp.sum(jnp.where(diagonal(values.shape[0]), values, 0.0), axis=0, keepdims=True)
+
+    gains_one, gains_zero = upright(gain1[...]), upright(gain0[...])
 
     def members(segment):
         return lax.broadcasted_iota(jnp.int32, (segments, segment.shape[1]), 0) == segment
@@ -148,15 +184,14 @@
         + highest(pick(rot[...], ptab.shape[0]), ptab[...])
         + highest(pick(cur[...], ctab.shape[0]), ctab[...])
     )
-    own[...] = seed * gain_row(seg1[...], gain1[...])
-    pl.semaphore_wait(barrier, 3)
+    own[...] = seed * gain_row(seg1[...], gains_one)
+    pl.semaphore_wait(barrier, n)
     pair_copy(own, peer, 0).start()
     mine = pl.ds(pl.multiple_of(case * local_cases, local_cases), local_cases)
     theirs = pl.ds(pl.multiple_of((1 - case) * local_cases, local_cases), local_cases)
     a_high[mine], a_low[mine] = split(own[...])
     column = jnp.sum(seed * f1[...], axis=0, keepdims=True)
-    picked = fold(jnp.where(members(seg1[...]), column, 0.0))
-    g1_out[...] = jnp.sum(picked, axis=1, keepdims=True)
+    g1[...] = fold(jnp.where(members(seg1[...]), column, 0.0))
     g0[...] = jnp.zeros_like(g0)
     total[...] = jnp.zeros_like(total)
     pair_copy(own, peer, 0).wait_recv()
@@ -192,7 +227,7 @@
         for d in range(2):
             start = pl.multiple_of(second_chunk(t, d) * width, width)
             segment = seg0[:, pl.ds(start, width)]
-            x_high, x_low = split(ring[n - 1 + t, d, rows] * gain_row(segment, gain0[...]))
+            x_high, x_low = split(ring[n - 1 + t, d, rows] * gain_row(segment, gains_zero))
             b_high, b_low = split(s0_buf[2 * t + d])
             total[rows] = total[rows] + dot3(x_high, x_low, b_high, b_low)
 
@@ -227,16 +262,33 @@
     lax.fori_loop(0, n - 1, gather_step, 0)
     for d in range(2):
         s0_copy(n - 1, d).wait()
+    gradient(n - 1)
+    pair_grads[0] = jnp.sum(g1[...], axis=1, keepdims=True) + jnp.zeros((segments, LANES), jnp.float32)
+    pair_grads[1] = jnp.sum(g0[...], axis=1, keepdims=True) + jnp.zeros((segments, LANES), jnp.float32)
+    grad_copy = pair_copy(pair_grads.at[pl.ds(0, 2)], pair_grads.at[pl.ds(2, 2)], 2)
+    grad_copy.start()
     second(n - 1, theirs)
     pair_copy(total.at[theirs], other, 1).start()
+    grad_copy.wait_recv()
+    row_grads[row] = pair_grads[pl.ds(0, 2)] + pair_grads[pl.ds(2, 2)]
+    for k in range(1, n):
+        row_copy(k).start()
     second(n - 1, mine)
-    gradient(n - 1)
-    g0_out[...] = jnp.sum(g0[...], axis=1, keepdims=True)
+    for k in range(1, n):
+        row_arrival(k).wait_recv()
+    grads = row_grads[0]
+    for k in range(1, n):
+        grads = grads + row_grads[k]
+    g1_out[...] = flat(grads[0, :, :1]) / cases
+    g0_out[...] = flat(grads[1, :, :1]) / cases
     pair_copy(total.at[theirs], other, 1).wait_recv()
     out[...] = total[mine] + other[...]
 
     pair_copy(own, peer, 0).wait_send()
     pair_copy(total.at[theirs], other, 1).wait_send()
+    grad_copy.wait_send()
+    for k in range(1, n):
+        row_copy(k).wait_send()
 
     def drain(step, carry):
         for d in range(2):
@@ -262,8 +314,8 @@
         functools.partial(ring_kernel, n),
         out_shape=(
             jax.ShapeDtypeStruct((local_cases, depth), f32),
-            jax.ShapeDtypeStruct((segments, 1), f32),
-            jax.ShapeDtypeStruct((segments, 1), f32),
+            jax.ShapeDtypeStruct((1, segments), f32),
+            jax.ShapeDtypeStruct((1, segments), f32),
         ),
         in_specs=[vmem] * 8 + [hbm] + [vmem] * 3 + [hbm],
         out_specs=(vmem, vmem, vmem),
@@ -279,12 +331,17 @@
             pltpu.VMEM((cases, depth), f32),
             pltpu.VMEM((local_cases, depth), f32),
             pltpu.VMEM((segments, LANES), f32),
+            pltpu.VMEM((segments, LANES), f32),
+            pltpu.VMEM((4, segments, LANES), f32),
+            pltpu.VMEM((n, 2, segments, LANES), f32),
             dma((2 * n - 1, 2, SUBS)),
             dma((2 * n - 1, 2, SUBS)),
             dma((2 * n,)),
             dma((2 * n,)),
-            dma((2,)),
-            dma((2,)),
+            dma((3,)),
+            dma((3,)),
+            dma((n,)),
+            dma((n,)),
         ],
         compiler_params=pltpu.CompilerParams(
             collective_id=0, has_side_effects=True, vmem_limit_bytes=62 * 1024 * 1024
@@ -293,8 +350,8 @@
             flops=12 * cases * depth * columns, bytes_accessed=12 * depth * columns, transcendentals=0
         ),
     )(
-        cot, rot[:, None], cur[:, None], ptab, ctab, seg1[None, :], gain1[:, None], f1, s1,
-        seg0[None, :], gain0[:, None], f0, s0,
+        cot, rot[None, :], cur[None, :], ptab, ctab, seg1[None, :], gain1[None, :], f1, s1,
+        seg0[None, :], gain0[None, :], f0, s0,
     )
 
 
@@ -302,32 +359,30 @@
     (cot, rot, cur, ptab, ctab, seg1, gain1, f1, s1, seg0, gain0, f0, s0) = args
     width = s1.shape[1] // (2 * n)
     if n % 2 == 0 and width % LANES == 0 and width * 2 * n == s1.shape[1]:
-        adjoint_zero, partial_one, partial_zero = ring_call(n, args)
-        partial_one, partial_zero = partial_one[:, 0], partial_zero[:, 0]
-        total_cases = 2 * cot.shape[0]
-    else:
-        highest = lax.Precision.HIGHEST
-        num_segments = gain1.shape[0]
-        adjoint_seed = cot + lookup(rot, ptab) + lookup(cur, ctab)
-        scaled_two = adjoint_seed * segment_rows(seg1, gain1)[None, :]
-        partial_one = segment_total(jnp.sum(adjoint_seed * f1, axis=0), seg1, num_segments)
-        all_seeds = lax.all_gather(scaled_two, "case", axis=0, tiled=True)
-        total_cases = all_seeds.shape[0]
-        own_adjoint = lax.psum_scatter(
-            jnp.dot(all_seeds, s1, precision=highest, preferred_element_type=jnp.float32),
-            "row",
-            scatter_dimension=0,
-            tiled=True,
-        )
-        scaled_one = own_adjoint * segment_rows(seg0, gain0)[None, :]
-        zero_terms = jnp.dot(
-            lax.all_gather(scaled_one, "row", axis=0, tiled=True),
-            s0,
-            precision=highest,
-            preferred_element_type=jnp.float32,
-        )
-        partial_zero = segment_total(jnp.sum(own_adjoint * f0, axis=0), seg0, num_segments)
-        adjoint_zero = lax.psum_scatter(zero_terms, "case", scatter_dimension=0, tiled=True)
+        adjoint_zero, grad_one, grad_zero = ring_call(n, args)
+        return adjoint_zero, grad_one[0], grad_zero[0]
+    highest = lax.Precision.HIGHEST
+    num_segments = gain1.shape[0]
+    adjoint_seed = cot + lookup(rot, ptab) + lookup(cur, ctab)
+    scaled_two = adjoint_seed * segment_rows(seg1, gain1)[None, :]
+    partial_one = segment_total(jnp.sum(adjoint_seed * f1, axis=0), seg1, num_segments)
+    all_seeds = lax.all_gather(scaled_two, "case", axis=0, tiled=True)
+    total_cases = all_seeds.shape[0]
+    own_adjoint = lax.psum_scatter(
+        jnp.dot(all_seeds, s1, precision=highest, preferred_element_type=jnp.float32),
+        "row",
+        scatter_dimension=0,
+        tiled=True,
+    )
+    scaled_one = own_adjoint * segment_rows(seg0, gain0)[None, :]
+    zero_terms = jnp.dot(
+        lax.all_gather(scaled_one, "row", axis=0, tiled=True),
+        s0,
+        precision=highest,
+        preferred_element_type=jnp.float32,
+    )
+    partial_zero = segment_total(jnp.sum(own_adjoint * f0, axis=0), seg0, num_segments)
+    adjoint_zero = lax.psum_scatter(zero_terms, "case", scatter_dimension=0, tiled=True)
     grad_one, grad_zero = lax.psum((partial_one, partial_zero), ("row", "case"))
     return (adjoint_zero, grad_one / total_cases, grad_zero / total_cases)
 

time: 179 us -> 153 us (0.85)
  blocking collectives: 32.9 us -> 0 us
  Pallas kernels: 135 us -> 147 us
  local copies, waits for them, and re-layouts: 7.65 us -> 4.3 us
  other arithmetic: 2.26 us -> 0 us
    psum x1 -> x0, blocking collectives: 32.9 us -> none  [local(): grad_one, grad_zero = lax.psum((partial_one, partial_zero), ('row', 'case'))]
    pallas_call x1, Pallas kernels: 135 us -> 147 us  [ring_call(): pl.pallas_call(functools.partial(ring_kernel, n), out_shape=(jax.ShapeDty...]
    broadcast_in_dim x4 -> x0, local copies, waits for them, and re-layouts: 5.57 us -> none  [the longest x1 1.44 us: ring_call(): rot[:, None]]
    unnamed x1 -> x3, local copies, waits for them, and re-layouts: 2.09 us -> 4.3 us
where the time goes in v2:
time: 153 us; the launch traced here: 152 us
  Pallas kernels  147 us (96%)
  local copies, waits for them, and re-layouts  4.3 us (3%)
    pallas_call x1, Pallas kernels, ring_call(): pl.pallas_call(functools.partial(ring_kernel, n), out_shape=(jax.ShapeDty...  147 us
    unnamed x3, local copies, waits for them, and re-layouts  4.3 us

profile of v2, /device:TPU:0, one launch (start us, length us, event | category | flops | bytes accessed | tf_op | source)
XLA Modules:
  0.0 151.8 jit_solution(7792684296595323035)
XLA Ops:
  0.6 146.9 %shard_map.148 = (f32[192,1024]{1,0:T(8,128)}, f32[1,64]{1,0:T(1,128)}, f32[1,64]{1,0:T(1,128)}) custom-call(f32[192,1024]{1,0:T(8,128)} %cot.1, s32[1,192]{1,0:T(1,128)} %bitcast.10, s32[1,192]{1,0:T(1,128)} %bitcast.11, f32[128,1024]{1,0:T(8,128)} %ptab.1, f32[16,1024]{1,0:T(8,128)} %ctab.1, s32[1,1024]{1,0:T(1,128)} %bitcast.9, f32[1,64]{1,0:T(1,128)} %bitcast.12, ...), custom_call_target="tpu_custom_call" | custom-call | flops 19327352832 | bytes 50331648 | tf_op jit(solution)/shard_map/pallas_call | solution.py:313
  147.5 2.1 %copy.19 = f32[192,1024]{1,0:T(8,128)} copy(f32[192,1024]{1,0:T(8,128)} %get-tuple-element.12) | data formatting | bytes 1572864
  149.6 1.1 copy.20
  150.7 1.1 copy.21

commit v3 on v2

--- a/solution.py
+++ b/solution.py
@@ -9,7 +9,7 @@
 
 MESH = pl.DeviceIdType.MESH
 LANES = 128
-SUBS = 4
+SUBS = 2
 
 
 def lookup(which, lookup_table):
@@ -211,20 +211,27 @@
             s0_copy(t, d).start()
 
     def reduce_step(step, carry):
-        for d in range(2):
-            part[d] = product(step, d)
+        now = lax.rem(step, 2)
         for h in range(SUBS):
             for d in range(2):
                 rows = pl.ds(h * sub, sub)
                 ring_copy(step - 1, d, h).wait_recv()
-                ring[step, d, rows] = ring[step, d, rows] + part[d, rows]
+                ring[step, d, rows] = ring[step, d, rows] + part[now, d, rows]
                 ring_copy(step, d, h).start()
+
+            @pl.when(step < n - 1)
+            def _():
+                part[1 - now, h] = product(step + 1, h)
+
         return carry
 
+    for d in range(2):
+        part[1, d] = product(1, d)
+
     lax.fori_loop(1, n, reduce_step, 0)
 
-    def second(t, rows):
-        for d in range(2):
+    def second(t, rows, directions=(0, 1)):
+        for d in directions:
             start = pl.multiple_of(second_chunk(t, d) * width, width)
             segment = seg0[:, pl.ds(start, width)]
             x_high, x_low = split(ring[n - 1 + t, d, rows] * gain_row(segment, gains_zero))
@@ -244,12 +251,12 @@
             g0[...] = g0[...] + fold(jnp.where(members(segment), column, 0.0))
 
     def gather_step(t, carry):
-        for d in range(2):
-            s0_copy(t, d).wait()
-        second(t, pl.ds(0, cases))
-        gradient(t)
         step = n + t
         for h in range(SUBS):
+            s0_copy(t, h).wait()
+            second(t, pl.ds(0, cases), (h,))
+            if h == 0:
+                gradient(t)
             for d in range(2):
                 ring_copy(step - 1, d, h).wait_recv()
 
@@ -327,7 +334,7 @@
             pltpu.VMEM((2 * n, depth, width), f32),
             pltpu.VMEM((2 * n, width, depth), f32),
             pltpu.VMEM((2 * n - 1, 2, cases, width), f32),
-            pltpu.VMEM((2, cases, width), f32),
+            pltpu.VMEM((2, 2, cases, width), f32),
             pltpu.VMEM((cases, depth), f32),
             pltpu.VMEM((local_cases, depth), f32),
             pltpu.VMEM((segments, LANES), f32),

time: 153 us -> 152 us (level)
  no operation moved by 1% of the time
where the time goes in v3:
time: 152 us; the launch traced here: 151 us
  Pallas kernels  146 us (96%)
  local copies, waits for them, and re-layouts  4.3 us (3%)
    pallas_call x1, Pallas kernels, ring_call(): pl.pallas_call(functools.partial(ring_kernel, n), out_shape=(jax.ShapeDty...  146 us
    unnamed x3, local copies, waits for them, and re-layouts  4.3 us

profile of v3, /device:TPU:0, one launch (start us, length us, event | category | flops | bytes accessed | tf_op | source)
XLA Modules:
  0.0 150.7 jit_solution(4646837092065171549)
XLA Ops:
  0.6 145.7 %shard_map.148 = (f32[192,1024]{1,0:T(8,128)}, f32[1,64]{1,0:T(1,128)}, f32[1,64]{1,0:T(1,128)}) custom-call(f32[192,1024]{1,0:T(8,128)} %cot.1, s32[1,192]{1,0:T(1,128)} %bitcast.10, s32[1,192]{1,0:T(1,128)} %bitcast.11, f32[128,1024]{1,0:T(8,128)} %ptab.1, f32[16,1024]{1,0:T(8,128)} %ctab.1, s32[1,1024]{1,0:T(1,128)} %bitcast.9, f32[1,64]{1,0:T(1,128)} %bitcast.12, ...), custom_call_target="tpu_custom_call" | custom-call | flops 19327352832 | bytes 50331648 | tf_op jit(solution)/shard_map/pallas_call | solution.py:320
  146.4 2.1 %copy.19 = f32[192,1024]{1,0:T(8,128)} copy(f32[192,1024]{1,0:T(8,128)} %get-tuple-element.12) | data formatting | bytes 1572864
  148.5 1.1 copy.20
  149.5 1.1 copy.21

commit v4 on v3

--- a/solution.py
+++ b/solution.py
@@ -270,14 +270,15 @@
     for d in range(2):
         s0_copy(n - 1, d).wait()
     gradient(n - 1)
-    pair_grads[0] = jnp.sum(g1[...], axis=1, keepdims=True) + jnp.zeros((segments, LANES), jnp.float32)
-    pair_grads[1] = jnp.sum(g0[...], axis=1, keepdims=True) + jnp.zeros((segments, LANES), jnp.float32)
-    grad_copy = pair_copy(pair_grads.at[pl.ds(0, 2)], pair_grads.at[pl.ds(2, 2)], 2)
+    pair_grads[0] = jnp.zeros(pair_grads.shape[1:], jnp.float32)
+    pair_grads[0, 0:1, :segments] = flat(jnp.sum(g1[...], axis=1, keepdims=True))
+    pair_grads[0, 1:2, :segments] = flat(jnp.sum(g0[...], axis=1, keepdims=True))
+    grad_copy = pair_copy(pair_grads.at[0], pair_grads.at[1], 2)
     grad_copy.start()
     second(n - 1, theirs)
     pair_copy(total.at[theirs], other, 1).start()
     grad_copy.wait_recv()
-    row_grads[row] = pair_grads[pl.ds(0, 2)] + pair_grads[pl.ds(2, 2)]
+    row_grads[row] = pair_grads[0] + pair_grads[1]
     for k in range(1, n):
         row_copy(k).start()
     second(n - 1, mine)
@@ -286,8 +287,8 @@
     grads = row_grads[0]
     for k in range(1, n):
         grads = grads + row_grads[k]
-    g1_out[...] = flat(grads[0, :, :1]) / cases
-    g0_out[...] = flat(grads[1, :, :1]) / cases
+    g1_out[...] = grads[0:1, :segments] / cases
+    g0_out[...] = grads[1:2, :segments] / cases
     pair_copy(total.at[theirs], other, 1).wait_recv()
     out[...] = total[mine] + other[...]
 
@@ -339,8 +340,8 @@
             pltpu.VMEM((local_cases, depth), f32),
             pltpu.VMEM((segments, LANES), f32),
             pltpu.VMEM((segments, LANES), f32),
-            pltpu.VMEM((4, segments, LANES), f32),
-            pltpu.VMEM((n, 2, segments, LANES), f32),
+            pltpu.VMEM((2, 8, pl.cdiv(segments, LANES) * LANES), f32),
+            pltpu.VMEM((n, 8, pl.cdiv(segments, LANES) * LANES), f32),
             dma((2 * n - 1, 2, SUBS)),
             dma((2 * n - 1, 2, SUBS)),
             dma((2 * n,)),

time: 152 us -> 144 us (0.947)
  Pallas kernels: 146 us -> 139 us
    pallas_call x1, Pallas kernels: 146 us -> 139 us  [ring_call(): pl.pallas_call(functools.partial(ring_kernel, n), out_shape=(jax.ShapeDty...]
where the time goes in v4:
time: 144 us
  Pallas kernels  139 us (97%)
  local copies, waits for them, and re-layouts  4.3 us (3%)
    pallas_call x1, Pallas kernels, ring_call(): pl.pallas_call(functools.partial(ring_kernel, n), out_shape=(jax.ShapeDty...  139 us
    unnamed x3, local copies, waits for them, and re-layouts  4.3 us

profile of v4, /device:TPU:0, one launch (start us, length us, event | category | flops | bytes accessed | tf_op | source)
XLA Modules:
  0.0 144.1 jit_solution(2102800853230066195)
XLA Ops:
  0.6 139.1 %shard_map.148 = (f32[192,1024]{1,0:T(8,128)}, f32[1,64]{1,0:T(1,128)}, f32[1,64]{1,0:T(1,128)}) custom-call(f32[192,1024]{1,0:T(8,128)} %cot.1, s32[1,192]{1,0:T(1,128)} %bitcast.10, s32[1,192]{1,0:T(1,128)} %bitcast.11, f32[128,1024]{1,0:T(8,128)} %ptab.1, f32[16,1024]{1,0:T(8,128)} %ctab.1, s32[1,1024]{1,0:T(1,128)} %bitcast.9, f32[1,64]{1,0:T(1,128)} %bitcast.12, ...), custom_call_target="tpu_custom_call" | custom-call | flops 19327352832 | bytes 50331648 | tf_op jit(solution)/shard_map/pallas_call | solution.py:321
  139.8 2.1 %copy.19 = f32[192,1024]{1,0:T(8,128)} copy(f32[192,1024]{1,0:T(8,128)} %get-tuple-element.12) | data formatting | bytes 1572864
  141.9 1.1 copy.20
  143.0 1.1 copy.21

commit v5 on v2

--- a/solution.py
+++ b/solution.py
@@ -9,7 +9,7 @@
 
 MESH = pl.DeviceIdType.MESH
 LANES = 128
-SUBS = 4
+SUBS = 2
 
 
 def lookup(which, lookup_table):
@@ -263,14 +263,15 @@
     for d in range(2):
         s0_copy(n - 1, d).wait()
     gradient(n - 1)
-    pair_grads[0] = jnp.sum(g1[...], axis=1, keepdims=True) + jnp.zeros((segments, LANES), jnp.float32)
-    pair_grads[1] = jnp.sum(g0[...], axis=1, keepdims=True) + jnp.zeros((segments, LANES), jnp.float32)
-    grad_copy = pair_copy(pair_grads.at[pl.ds(0, 2)], pair_grads.at[pl.ds(2, 2)], 2)
+    pair_grads[0] = jnp.zeros(pair_grads.shape[1:], jnp.float32)
+    pair_grads[0, 0:1, :segments] = flat(jnp.sum(g1[...], axis=1, keepdims=True))
+    pair_grads[0, 1:2, :segments] = flat(jnp.sum(g0[...], axis=1, keepdims=True))
+    grad_copy = pair_copy(pair_grads.at[0], pair_grads.at[1], 2)
     grad_copy.start()
     second(n - 1, theirs)
     pair_copy(total.at[theirs], other, 1).start()
     grad_copy.wait_recv()
-    row_grads[row] = pair_grads[pl.ds(0, 2)] + pair_grads[pl.ds(2, 2)]
+    row_grads[row] = pair_grads[0] + pair_grads[1]
     for k in range(1, n):
         row_copy(k).start()
     second(n - 1, mine)
@@ -279,8 +280,8 @@
     grads = row_grads[0]
     for k in range(1, n):
         grads = grads + row_grads[k]
-    g1_out[...] = flat(grads[0, :, :1]) / cases
-    g0_out[...] = flat(grads[1, :, :1]) / cases
+    g1_out[...] = grads[0:1, :segments] / cases
+    g0_out[...] = grads[1:2, :segments] / cases
     pair_copy(total.at[theirs], other, 1).wait_recv()
     out[...] = total[mine] + other[...]
 
@@ -332,8 +333,8 @@
             pltpu.VMEM((local_cases, depth), f32),
             pltpu.VMEM((segments, LANES), f32),
             pltpu.VMEM((segments, LANES), f32),
-            pltpu.VMEM((4, segments, LANES), f32),
-            pltpu.VMEM((n, 2, segments, LANES), f32),
+            pltpu.VMEM((2, 8, pl.cdiv(segments, LANES) * LANES), f32),
+            pltpu.VMEM((n, 8, pl.cdiv(segments, LANES) * LANES), f32),
             dma((2 * n - 1, 2, SUBS)),
             dma((2 * n - 1, 2, SUBS)),
             dma((2 * n,)),

time: 153 us -> 144 us (0.941)
  Pallas kernels: 147 us -> 139 us
    pallas_call x1, Pallas kernels: 147 us -> 139 us  [ring_call(): pl.pallas_call(functools.partial(ring_kernel, n), out_shape=(jax.ShapeDty...]
where the time goes in v5:
time: 144 us
  Pallas kernels  139 us (97%)
  local copies, waits for them, and re-layouts  4.3 us (3%)
    pallas_call x1, Pallas kernels, ring_call(): pl.pallas_call(functools.partial(ring_kernel, n), out_shape=(jax.ShapeDty...  139 us
    unnamed x3, local copies, waits for them, and re-layouts  4.3 us

profile of v5, /device:TPU:0, one launch (start us, length us, event | category | flops | bytes accessed | tf_op | source)
XLA Modules:
  0.0 144.1 jit_solution(7645729293808028538)
XLA Ops:
  0.6 139.1 %shard_map.148 = (f32[192,1024]{1,0:T(8,128)}, f32[1,64]{1,0:T(1,128)}, f32[1,64]{1,0:T(1,128)}) custom-call(f32[192,1024]{1,0:T(8,128)} %cot.1, s32[1,192]{1,0:T(1,128)} %bitcast.10, s32[1,192]{1,0:T(1,128)} %bitcast.11, f32[128,1024]{1,0:T(8,128)} %ptab.1, f32[16,1024]{1,0:T(8,128)} %ctab.1, s32[1,1024]{1,0:T(1,128)} %bitcast.9, f32[1,64]{1,0:T(1,128)} %bitcast.12, ...), custom_call_target="tpu_custom_call" | custom-call | flops 19327352832 | bytes 50331648 | tf_op jit(solution)/shard_map/pallas_call | solution.py:314
  139.8 2.1 %copy.19 = f32[192,1024]{1,0:T(8,128)} copy(f32[192,1024]{1,0:T(8,128)} %get-tuple-element.12) | data formatting | bytes 1572864
  141.9 1.1 copy.20
  143.0 1.1 copy.21
